TPU v7x, 128 devices: a whole 4x4x4 slice. The times are simulated.
128 devices in a mesh: bins: 8 (over y, core), space: 16 (over z, x).
Axes of the slice: x: 4, y: 4, z: 4, core: 2. Of those that a mesh axis runs over, the one named last changes fastest.
Arguments:
- spectra: float32 [1152, 1024, 128], P('bins', 'space'), may hold values from 0.05 to 2
- land_mask: int32 [1024, 128], P('space'), may hold values 0 or 1
- growth: float32 [1152], replicated, may hold values from 0.1 to 1
- band_weight: float32 [1152], replicated, may hold values from 0.00043402778 to 0.0034722222
- kernel_gain: bfloat16 [1152, 1152], replicated, may hold values from -0.1875 to 0.1875
- kernel_loss: bfloat16 [1152, 1152], replicated, may hold values from -0.1875 to 0.1875
Outputs:
- updated: float32 [1152, 1024, 128], P('bins', 'space')
All inputs are finite; a program needn't handle non-finite values. No bound on the sum of `land_mask` on one device may be relied on, other than what follows from the above.
Results may differ from a plain program's by a relative error of at most 0.00056.
Values sent between devices are 32-bit elements; how exact they have to be, the bound alone decides.
A program may use at most 64 MiB of HBM per device.

v0:
```python
import math

import jax
import jax.numpy as jnp
from jax import lax
from jax.sharding import PartitionSpec as P

NF = 32
ND = 36
SUBSTEPS = 4


def extended(cells, sides, width):
    for axis, dim in sides:
        count = lax.axis_size(axis)
        ends = count - 1
        head = lax.slice_in_dim(cells, 0, width, axis=dim)
        tail = lax.slice_in_dim(cells, cells.shape[dim] - width, cells.shape[dim], axis=dim)
        cells = jnp.concatenate(
            [
                lax.ppermute(tail, axis, [(i, (i + 1) % count) for i in range(ends)]),
                cells,
                lax.ppermute(head, axis, [((i + 1) % count, i) for i in range(ends)]),
            ],
            axis=dim,
        )
    return cells


def courants(first, count):
    index = first + jnp.arange(count, dtype=jnp.int32)
    freq = (index // ND).astype(jnp.float32)
    direc = (index % ND).astype(jnp.float32)
    group = 1.0 / (1.0 + 2.3 * freq / max(NF - 1, 1))
    theta = 2.0 * math.pi * (direc + 0.5) / ND
    return (0.9 * group * jnp.cos(theta), 0.9 * group * jnp.sin(theta))


def along_rows(padded, speed):
    plus = jnp.maximum(speed, 0.0)
    minus = jnp.maximum(-speed, 0.0)
    middle = padded[:, 1:-1]
    return middle - plus * (middle - padded[:, :-2]) - minus * (middle - padded[:, 2:])


def along_columns(field, speed):
    plus = jnp.maximum(speed, 0.0)
    minus = jnp.maximum(-speed, 0.0)
    padded = jnp.pad(field, ((0, 0), (0, 0), (1, 1)))
    return field - plus * (field - padded[:, :, :-2]) - minus * (field - padded[:, :, 2:])


def sources(block, growth, band_weight, kernel_gain, kernel_loss):
    state = block.astype(jnp.bfloat16)
    square = (block * block).astype(jnp.bfloat16)
    gain = jnp.dot(kernel_gain, state, preferred_element_type=jnp.float32)
    loss = jnp.dot(kernel_loss, square, preferred_element_type=jnp.float32)
    energy = jnp.sum(band_weight[:, None] * block, axis=0)
    return (block + 0.25 * (growth[:, None] * block + block * gain - loss)) / (1.0 + 0.5 * energy)


def local(spectra, land_mask, growth, band_weight, kernel_gain, kernel_loss):
    local_bins, rows, columns = spectra.shape
    first = lax.axis_index("bins") * local_bins
    speed_x, speed_y = courants(first, local_bins)
    speed_x = speed_x[:, None, None]
    speed_y = speed_y[:, None, None]
    sea = land_mask.astype(jnp.float32)
    field = spectra
    padded = extended(field, (("space", 1),), SUBSTEPS)
    sea_wide = extended(sea, (("space", 0),), SUBSTEPS)
    for step in range(SUBSTEPS):
        padded = along_rows(padded, speed_x)
        sea_wide = sea_wide[1:-1]
        padded = sea_wide[None] * along_columns(padded, speed_y)
    field = padded
    points = rows * columns
    flat = field.reshape(local_bins, points)
    whole = lax.all_to_all(flat, "bins", split_axis=1, concat_axis=0, tiled=True)
    fresh = sources(whole, growth, band_weight, kernel_gain, kernel_loss)
    back = lax.all_to_all(fresh, "bins", split_axis=0, concat_axis=1, tiled=True)
    back = back.reshape(local_bins, rows, columns)
    return sea[None] * back


def solution(mesh):
    in_specs = (P("bins", "space", None), P("space", None), P(), P(), P(), P())
    out_specs = P("bins", "space", None)
    return jax.shard_map(local, mesh=mesh, in_specs=in_specs, out_specs=out_specs, check_vma=False)
```

profile of v0, /device:TPU:1, one launch (start us, length us, event | category | flops | bytes accessed | tf_op | source)
XLA Modules:
  0.0 228.4 jit_solution(9661974090947251840)
XLA Ops:
  0.0 0.0 copy-start
  0.0 0.9 convert_element_type.49
  0.9 3.9 %collective-permute-start = (f32[4,128]{1,0:T(4,128)S(1)}, f32[4,128]{1,0:T(4,128)S(1)}, u32[]{:S(2)}, u32[]{:S(2)}) collective-permute-start(f32[4,128]{1,0:T(4,128)S(1)} %get-tuple-element.7), channel_id=1, source_target_pairs={{0,1},{1,2},{2,3},{3,4},{4,5},{5,6},{6,7},{7,8},{8,9},{9,10},{10,1... | collective-permute-start | bytes 6152 | tf_op jit(solution)/shard_map/ppermute | solution.py:21
  4.9 1.3 collective-permute-start.1
  6.2 1.4 fusion.55
  7.5 4.7 %collective-permute-start.2 = (f32[144,4,128]{2,1,0:T(4,128)S(1)}, f32[144,4,128]{2,1,0:T(4,128)}, u32[]{:S(2)}, u32[]{:S(2)}) collective-permute-start(f32[144,4,128]{2,1,0:T(4,128)S(1)} %get-tuple-element.5), channel_id=1, source_target_pairs={{0,1},{1,2},{2,3},{3,4},{4,5},{5,6},{6,7},{7,8},{8,9},{9,10},{10,1... | collective-permute-start | bytes 884744 | tf_op jit(solution)/shard_map/ppermute | solution.py:21
  12.2 1.3 collective-permute-start.3
  13.5 0.1 negate_maximum_fusion
  13.6 0.1 broadcast_maximum_fusion
  13.6 0.0 collective-permute-done
  13.7 0.0 collective-permute-done.1
  13.7 2.8 %collective-permute-done.2 = f32[144,4,128]{2,1,0:T(4,128)} collective-permute-done((f32[144,4,128]{2,1,0:T(4,128)S(1)}, f32[144,4,128]{2,1,0:T(4,128)}, u32[]{:S(2)}, u32[]{:S(2)}) %collective-permute-start.2) | collective-permute-done | bytes 294944 | tf_op jit(solution)/shard_map/ppermute | solution.py:21
  16.6 4.6 %collective-permute-done.3 = f32[144,4,128]{2,1,0:T(4,128)} collective-permute-done((f32[144,4,128]{2,1,0:T(4,128)S(1)}, f32[144,4,128]{2,1,0:T(4,128)}, u32[]{:S(2)}, u32[]{:S(2)}) %collective-permute-start.3) | collective-permute-done | bytes 294944 | tf_op jit(solution)/shard_map/ppermute | solution.py:23
  21.2 3.1 %pad_maximum_fusion = f32[144,72,128]{2,1,0:T(8,128)S(1)} fusion(f32[144,4,128]{2,1,0:T(4,128)} %collective-permute-done.3, f32[144,64,128]{2,1,0:T(8,128)} %param.6, f32[144,4,128]{2,1,0:T(4,128)} %collective-permute-done.2), kind=kLoop, calls=%fused_computation.47 | loop fusion | flops 2654208 | bytes 10616832 | tf_op jit(solution)/shard_map/concatenate | solution.py:19
  24.3 2.0 fusion.30
  26.3 3.8 %fusion.4 = f32[144,70,128]{2,1,0:T(8,128)S(1)} fusion(f32[144,70,128]{2,1,0:T(8,128)S(1)} %fusion.30, f32[144]{0:T(256)S(1)} %get-tuple-element.9, f32[144]{0:T(256)S(1)} %get-tuple-element.11, f32[70,128]{1,0:T(8,128)S(1)} %slice.116), kind=kLoop, calls=%fused_computation.12 | loop fusion | flops 9031680 | bytes 10358912 | tf_op jit(solution)/shard_map/mul | solution.py:75
  30.1 2.0 fusion.26
  32.1 3.8 %fusion.11 = f32[144,68,128]{2,1,0:T(8,128)S(1)} fusion(f32[144,68,128]{2,1,0:T(8,128)S(1)} %fusion.26, f32[144]{0:T(256)S(1)} %get-tuple-element.9, f32[144]{0:T(256)S(1)} %get-tuple-element.11, f32[68,128]{1,0:T(8,128)S(1)} %slice.115), kind=kLoop, calls=%fused_computation.19 | loop fusion | flops 8773632 | bytes 10062976 | tf_op jit(solution)/shard_map/mul | solution.py:75
  35.9 2.0 fusion.22
  37.9 3.8 %fusion.18 = f32[144,66,128]{2,1,0:T(8,128)S(1)} fusion(f32[144,66,128]{2,1,0:T(8,128)S(1)} %fusion.22, f32[144]{0:T(256)S(1)} %get-tuple-element.9, f32[144]{0:T(256)S(1)} %get-tuple-element.11, f32[66,128]{1,0:T(8,128)S(1)} %slice.114), kind=kLoop, calls=%fused_computation.26 | loop fusion | flops 8515584 | bytes 9767040 | tf_op jit(solution)/shard_map/mul | solution.py:75
  41.7 1.8 fusion.41
  43.5 5.0 %fusion.37 = f32[144,64,128]{2,1,0:T(8,128)} fusion(f32[144,64,128]{2,1,0:T(8,128)S(1)} %fusion.41, f32[144]{0:T(256)S(1)} %get-tuple-element.9, f32[144]{0:T(256)S(1)} %get-tuple-element.11, f32[64,128]{1,0:T(8,128)S(1)} %convert_element_type.49), kind=kLoop, calls=%fused_computation.52 | loop fusion | flops 8257536 | bytes 9471104 | tf_op jit(solution)/shard_map/mul | solution.py:75
  48.6 5.9 %all_to_all.26 = f32[144,8,1024]{2,1,0:T(8,128)} reshape(f32[144,64,128]{2,1,0:T(8,128)} %fusion.37) | data formatting | bytes 9437184 | tf_op jit(solution)/shard_map/all_to_all | solution.py:79
  54.5 7.3 %copy.23 = f32[144,8,1024]{2,0,1:T(8,128)} copy(f32[144,8,1024]{2,1,0:T(8,128)} %all_to_all.26) | data formatting | bytes 9437184 | tf_op jit(solution)/shard_map/all_to_all | solution.py:79
  61.8 0.0 copy-start.2
  61.8 7.1 %all-to-all-start = ((f32[144,8,1024]{2,0,1:T(8,128)}), f32[144,8,1024]{2,0,1:T(8,128)}, u32[]{:S(2)}, u32[]{:S(2)}) async-start(f32[144,8,1024]{2,0,1:T(8,128)} %copy.23), calls=%async_computation | async-start | bytes 9437184 | tf_op jit(solution)/shard_map/all_to_all | solution.py:79
  68.8 0.0 copy-done.2
  68.8 0.1 mul.305
  68.9 54.5 %all-to-all-done = f32[144,8,1024]{2,0,1:T(8,128)} async-done(((f32[144,8,1024]{2,0,1:T(8,128)}), f32[144,8,1024]{2,0,1:T(8,128)}, u32[]{:S(2)}, u32[]{:S(2)}) %all-to-all-start) | async-done | bytes 4718624 | tf_op jit(solution)/shard_map/all_to_all | solution.py:79
  123.4 2.7 %fusion.47 = f32[1024]{0:T(1024)S(1)} fusion(f32[144,8,1024]{2,0,1:T(8,128)} %all-to-all-done, f32[8,144]{1,0:T(8,128)S(1)} %mul.305), kind=kLoop, calls=%fused_computation.67 | loop fusion | flops 2358272 | bytes 4727296 | tf_op jit(solution)/shard_map/reduce_sum | solution.py:58
  126.1 6.0 %copy.25 = f32[1152,1024]{0,1:T(8,128)} copy(f32[1152,1024]{1,0:T(8,128)} %bitcast.1) | data formatting | bytes 9437184 | tf_op jit(solution)/shard_map/all_to_all | solution.py:79
  132.2 0.0 copy-done
  132.2 0.0 copy-start.1
  132.2 0.0 copy-start.3
  132.2 0.0 copy-start.4
  132.2 5.7 %fusion.48 = f32[1024,1152]{1,0:T(8,128)S(1)} fusion(bf16[1152,1152]{1,0:T(8,128)(2,1)S(1)} %copy-done, f32[1152,1024]{1,0:T(8,128)} %bitcast.1), kind=kOutput, calls=%fused_computation.69 | convolution fusion | flops 2720268288 | bytes 12091392 | tf_op jit(solution)/shard_map/dot_general | solution.py:57
  137.9 0.0 copy-done.1
  137.9 0.0 copy-done.3
  137.9 0.0 copy-done.4
  137.9 8.6 %fusion.46 = f32[1152,1024]{0,1:T(8,128)} fusion(f32[1152,1024]{0,1:T(8,128)S(1)} %copy-done.1, f32[1024,1152]{1,0:T(8,128)S(1)} %fusion.48, bf16[1152,1152]{1,0:T(8,128)(2,1)S(1)} %copy-done.3, f32[1152]{0:T(1024)S(1)} %copy-done.4, f32[1024]{0:T(1024)S(1)} %multiply_add_fusion, f32[1152,1024]{1,0:T(8,128)} %bitcast.1), kind=kOutput, calls=%fused_computation.64 | convolution fusion | flops 2726166528 | bytes 21537280 | tf_op jit(solution)/shard_map/dot_general | solution.py:56
  146.5 6.0 %copy.26 = f32[1152,1024]{1,0:T(8,128)} copy(f32[1152,1024]{0,1:T(8,128)} %fusion.46) | data formatting | bytes 9437184 | tf_op jit(solution)/shard_map/div | solution.py:59
  152.6 59.5 %all_to_all.35 = f32[8,144,1024]{2,1,0:T(8,128)S(1)} all-to-all(f32[8,144,1024]{2,1,0:T(8,128)} %bitcast.22), channel_id=1, replica_groups=mesh['bins'=8,'space'=16] {'bins'}, dimensions={0} | all-to-all | bytes 9437184 | tf_op jit(solution)/shard_map/all_to_all | solution.py:81
  212.1 4.9 %copy.27 = f32[144,8,1024]{2,1,0:T(8,128)} copy(f32[144,8,1024]{2,0,1:T(8,128)S(1)} %bitcast.23) | data formatting | bytes 9437184 | tf_op jit(solution)/shard_map/all_to_all | solution.py:81
  217.0 5.9 %reshape.74 = f32[144,64,128]{2,1,0:T(8,128)} reshape(f32[144,8,1024]{2,1,0:T(8,128)} %copy.27) | data formatting | bytes 9437184 | tf_op jit(solution)/shard_map/reshape | solution.py:82
  222.9 5.5 %broadcast_multiply_fusion = f32[144,64,128]{2,1,0:T(8,128)} fusion(f32[144,64,128]{2,1,0:T(8,128)} %reshape.74, f32[64,128]{1,0:T(8,128)S(1)} %convert_element_type.49), kind=kLoop, calls=%fused_computation.71 | loop fusion | flops 1179648 | bytes 9469952 | tf_op jit(solution)/shard_map/mul | solution.py:83
  (6 shorter events, 0.0 us)
Async XLA Ops:
  0.0 132.2 %copy-start = (bf16[1152,1152]{1,0:T(8,128)(2,1)S(1)}, bf16[1152,1152]{1,0:T(8,128)(2,1)}, u32[]{:S(2)}) copy-start(bf16[1152,1152]{1,0:T(8,128)(2,1)} %param.11) | copy-start | bytes 7962628
  0.9 12.7 %collective-permute-start = (f32[4,128]{1,0:T(4,128)S(1)}, f32[4,128]{1,0:T(4,128)S(1)}, u32[]{:S(2)}, u32[]{:S(2)}) collective-permute-start(f32[4,128]{1,0:T(4,128)S(1)} %get-tuple-element.7), channel_id=1, source_target_pairs={{0,1},{1,2},{2,3},{3,4},{4,5},{5,6},{6,7},{7,8},{8,9},{9,10},{10,1... | collective-permute-start | bytes 6152 | tf_op jit(solution)/shard_map/ppermute | solution.py:21
  4.9 8.8 %collective-permute-start.1 = (f32[4,128]{1,0:T(4,128)S(1)}, f32[4,128]{1,0:T(4,128)S(1)}, u32[]{:S(2)}, u32[]{:S(2)}) collective-permute-start(f32[4,128]{1,0:T(4,128)S(1)} %get-tuple-element.8), channel_id=1, source_target_pairs={{1,0},{2,1},{3,2},{4,3},{5,4},{6,5},{7,6},{8,7},{9,8},{10,9},{11,1... | collective-permute-start | bytes 6152 | tf_op jit(solution)/shard_map/ppermute | solution.py:23
  7.5 9.0 %collective-permute-start.2 = (f32[144,4,128]{2,1,0:T(4,128)S(1)}, f32[144,4,128]{2,1,0:T(4,128)}, u32[]{:S(2)}, u32[]{:S(2)}) collective-permute-start(f32[144,4,128]{2,1,0:T(4,128)S(1)} %get-tuple-element.5), channel_id=1, source_target_pairs={{0,1},{1,2},{2,3},{3,4},{4,5},{5,6},{6,7},{7,8},{8,9},{9,10},{10,1... | collective-permute-start | bytes 884744 | tf_op jit(solution)/shard_map/ppermute | solution.py:21
  12.2 9.0 %collective-permute-start.3 = (f32[144,4,128]{2,1,0:T(4,128)S(1)}, f32[144,4,128]{2,1,0:T(4,128)}, u32[]{:S(2)}, u32[]{:S(2)}) collective-permute-start(f32[144,4,128]{2,1,0:T(4,128)S(1)} %get-tuple-element.6), channel_id=1, source_target_pairs={{1,0},{2,1},{3,2},{4,3},{5,4},{6,5},{7,6},{8,7},{9,8},{10,9},{11,1... | collective-permute-start | bytes 884744 | tf_op jit(solution)/shard_map/ppermute | solution.py:23
  61.8 7.1 %copy-start.2 = (f32[1152]{0:T(1024)S(1)}, f32[1152]{0:T(1024)}, u32[]{:S(2)}) copy-start(f32[1152]{0:T(1024)} %param.9) | copy-start | bytes 13828
  61.8 61.6 %all-to-all-start = ((f32[144,8,1024]{2,0,1:T(8,128)}), f32[144,8,1024]{2,0,1:T(8,128)}, u32[]{:S(2)}, u32[]{:S(2)}) async-start(f32[144,8,1024]{2,0,1:T(8,128)} %copy.23), calls=%async_computation | async-start | bytes 9437184 | tf_op jit(solution)/shard_map/all_to_all | solution.py:79
  132.2 5.7 %copy-start.1 = (f32[1152,1024]{0,1:T(8,128)S(1)}, f32[1152,1024]{0,1:T(8,128)}, u32[]{:S(2)}) copy-start(f32[1152,1024]{0,1:T(8,128)} %copy.25) | copy-start | bytes 14155780
  132.2 5.7 %copy-start.3 = (bf16[1152,1152]{1,0:T(8,128)(2,1)S(1)}, bf16[1152,1152]{1,0:T(8,128)(2,1)}, u32[]{:S(2)}) copy-start(bf16[1152,1152]{1,0:T(8,128)(2,1)} %param.10) | copy-start | bytes 7962628
  132.2 5.7 %copy-start.4 = (f32[1152]{0:T(1024)S(1)}, f32[1152]{0:T(1024)}, u32[]{:S(2)}) copy-start(f32[1152]{0:T(1024)} %param.8) | copy-start | bytes 13828
where the time goes:
time: 233 us; the launch traced here: 228 us
  waiting for transfers between devices  61.9 us (27%)
  blocking collectives  59.5 us (26%)
  local copies, waits for them, and re-layouts  37.6 us (16%)
  other arithmetic  36.6 us (16%)
  starting transfers between devices  18.3 us (8%)
  matrix products  14.3 us (6%)
    all_to_all x1, blocking collectives, local(): lax.all_to_all(fresh, 'bins', split_axis=0, concat_axis=1, tiled=True)  59.5 us
    all_to_all x1, waiting for transfers between devices, local(): lax.all_to_all(flat, 'bins', split_axis=1, concat_axis=0, tiled=True)  54.5 us
    all_to_all x3, local copies, waits for them, and re-layouts, local(): lax.all_to_all(flat, 'bins', split_axis=1, concat_axis=0, tiled=True)  19.2 us
    mul x4, other arithmetic, local(): padded = sea_wide[None] * along_columns(padded, speed_y)  16.4 us
    dot_general x1, matrix products, sources(): gain = jnp.dot(kernel_gain, state, preferred_element_type=jnp.float32)  8.64 us
    ppermute x2, starting transfers between devices, extended(): lax.ppermute(tail, axis, [(i, (i + 1) % count) for i in range(ends)])  8.64 us
    sub x4, other arithmetic, along_rows(): middle - plus * (middle - padded[:, :-2]) - minus * (middle - padded[:, 2:])  7.89 us
    all_to_all x1, starting transfers between devices, local(): lax.all_to_all(flat, 'bins', split_axis=1, concat_axis=0, tiled=True)  7.05 us
  transfers between devices with their start and end apart: 5, of which 3 were waited for; matrix products, arithmetic and copies ran while one was open for 1% of the time, Pallas kernels for 0%

commit v1 on v0

v1 whole, which is shorter than its diff:
```python
import functools
import math

import jax
import jax.numpy as jnp
import numpy as np
from jax import lax
from jax.experimental import pallas as pl
from jax.experimental.pallas import tpu as pltpu
from jax.sharding import PartitionSpec as P

NF = 32
ND = 36
SUBSTEPS = 4
PEERS = 8
SLABS = 16
LB = 144
NB = 1152
ROWS = 64
COLS = 128
PAD = ROWS + 16
ROUNDS = 8
MESH = pl.DeviceIdType.MESH


def device_of(slot):
    return (slot % 4) * 2 + slot // 4


def slot_of(device):
    return device // 2 + 4 * lax.rem(device, 2)


def kernel(x, mask, cosv, sinv, grow, band, kg, kl, out,
           fin, seab, mlo, mhi, sent, got, fresh, back, outv, kgv, klv, growb, bandb, state, square,
           load_sem, halo_send, halo_recv, own_sem, fs, fr, bs, br, out_sem):
    me = lax.axis_index("bins")
    space = lax.axis_index("space")
    up = lax.rem(space + 1, SLABS)
    down = lax.rem(space + SLABS - 1, SLABS)

    barrier = pltpu.get_barrier_semaphore()
    for i in range(1, PEERS):
        pl.semaphore_signal(barrier, inc=1, device_id=(lax.rem(me + i, PEERS), space), device_id_type=MESH)
    for other in (up, down):
        pl.semaphore_signal(barrier, inc=1, device_id=(me, other), device_id_type=MESH)

    def load(q):
        return pltpu.make_async_copy(x.at[:, pl.ds(8 * q, 8), :], fin.at[:, pl.ds(8 * q + 8, 8), :], load_sem.at[q])

    for q in (1, 2, 3, 4, 5, 6, 0, 7):
        load(q).start()
    weights = [pltpu.make_async_copy(kg, kgv, load_sem.at[8]), pltpu.make_async_copy(kl, klv, load_sem.at[9])]

    for q in range(ROWS // 8):
        sea = mask[8 * q:8 * q + 8, :].astype(jnp.float32)
        for i in range(8):
            seab[8 + 8 * q + i] = jnp.broadcast_to(sea[i:i + 1, :], (8, COLS))

    halos = [
        pltpu.make_async_remote_copy(x.at[:, pl.ds(56, 8), :], fin.at[:, pl.ds(0, 8), :], halo_send.at[0], halo_recv.at[0],
                                     device_id=(me, up), device_id_type=MESH),
        pltpu.make_async_remote_copy(x.at[:, pl.ds(0, 8), :], fin.at[:, pl.ds(72, 8), :], halo_send.at[1], halo_recv.at[1],
                                     device_id=(me, down), device_id_type=MESH),
        pltpu.make_async_remote_copy(mask.at[pl.ds(56, 8), :], mlo, halo_send.at[2], halo_recv.at[2],
                                     device_id=(me, up), device_id_type=MESH),
        pltpu.make_async_remote_copy(mask.at[pl.ds(0, 8), :], mhi, halo_send.at[3], halo_recv.at[3],
                                     device_id=(me, down), device_id_type=MESH),
    ]
    inside_lo = (space > 0).astype(jnp.float32)
    inside_hi = (space < SLABS - 1).astype(jnp.float32)
    flat = fin.reshape(LB * PAD, COLS)
    lane = lax.broadcasted_iota(jnp.int32, (8, COLS), 1)
    sub = lax.broadcasted_iota(jnp.int32, (8, COLS), 0)

    def propagate(g):
        def tile(t, carry):
            b0 = pl.multiple_of(t * 8, 8)
            rows = [flat[pl.ds(b0 * PAD + 16 * g + 4 + i, 8, stride=PAD), :] for i in range(24)]
            if g == 0:
                rows = [r * inside_lo for r in rows[:4]] + rows[4:]
            if g == 3:
                rows = rows[:20] + [r * inside_hi for r in rows[20:]]
            field = jnp.stack(rows)
            b = sub + b0
            one = lambda c: c.astype(jnp.float32)
            freq = (4 * me).astype(jnp.float32) + one(b >= ND) + one(b >= 2 * ND) + one(b >= 3 * ND)
            group = 0.9 / (1.0 + 2.3 * freq / max(NF - 1, 1))
            cx = group * cosv[pl.ds(b0, 8), :]
            cy = group * sinv[pl.ds(b0, 8), :]
            right, ahead = cx > 0.0, cy > 0.0
            ax, ay = jnp.abs(cx), jnp.abs(cy)
            stay = 1.0 - ay
            move = jnp.where((ahead & (lane == 0)) | (~ahead & (lane == COLS - 1)), 0.0, ay)
            for step in range(SUBSTEPS):
                n = field.shape[0] - 2
                mid = field[1:-1]
                near = jnp.where(right[None], field[:-2], field[2:])
                mid = mid + ax[None] * (near - mid)
                near = jnp.stack([jnp.where(ahead, pltpu.roll(mid[i], 1, 1), pltpu.roll(mid[i], COLS - 1, 1)) for i in range(n)])
                field = (stay[None] * mid + move[None] * near) * seab[pl.ds(16 * g + 5 + step, n)]
            sent[pl.ds(16 * g, 16), pl.ds(b0, 8), :] = field
            return carry
        lax.fori_loop(0, LB // 8, tile, 0)

    def forward(j, d):
        row = 8 * j + slot_of(d)
        return pltpu.make_async_remote_copy(
            sent.at[row], got.at[j, pl.ds(me * LB, LB), :], fs.at[j, d], fr.at[j, me],
            device_id=(d, space), device_id_type=MESH)

    def arrival(j, d):
        return pltpu.make_async_remote_copy(
            sent.at[0], got.at[j, pl.ds(d * LB, LB), :], fs.at[j, d], fr.at[j, d],
            device_id=(d, space), device_id_type=MESH)

    def own(j):
        return pltpu.make_async_copy(sent.at[8 * j + slot_of(me)], got.at[j, pl.ds(me * LB, LB), :], own_sem.at[0, j])

    def give(j, d):
        return pltpu.make_async_remote_copy(
            fresh.at[j, pl.ds(d * LB, LB), :], back.at[pl.ds((8 * j + slot_of(me)) * LB, LB), :], bs.at[j, d], br.at[j, me],
            device_id=(d, space), device_id_type=MESH)

    def returned(j, d):
        return pltpu.make_async_remote_copy(
            fresh.at[j, pl.ds(d * LB, LB), :], back.at[pl.ds((8 * j + slot_of(d)) * LB, LB), :], bs.at[j, d], br.at[j, d],
            device_id=(d, space), device_id_type=MESH)

    def keep(j):
        return pltpu.make_async_copy(
            fresh.at[j, pl.ds(me * LB, LB), :], back.at[pl.ds((8 * j + slot_of(me)) * LB, LB), :], own_sem.at[1, j])

    def others(body):
        def step(i, carry):
            body(lax.rem(me + i, PEERS))
            return carry
        lax.fori_loop(1, PEERS, step, 0)

    ready = set()
    first = True
    for g in (1, 2, 0, 3):
        for q in range(max(2 * g - 1, 0), min(2 * g + 3, 8)):
            if q not in ready:
                load(q).wait()
                ready.add(q)
        if g == 0:
            for h in halos:
                h.wait_recv()
            for q, (ref, inside) in ((0, (mlo, inside_lo)), (72, (mhi, inside_hi))):
                sea = ref[...].astype(jnp.float32) * inside
                for i in range(8):
                    seab[q + i] = jnp.broadcast_to(sea[i:i + 1, :], (8, COLS))
        propagate(g)
        if first:
            pl.semaphore_wait(barrier, PEERS + 1)
            for h in halos:
                h.start()
            first = False
        for j in (2 * g, 2 * g + 1):
            others(lambda d: forward(j, d).start())
            own(j).start()
        if g == 2:
            for w in weights:
                w.start()
            for i in range(NB // COLS):
                at = pl.ds(i * COLS, COLS)
                growb[at, :] = jnp.transpose(jnp.broadcast_to(0.25 * grow[i:i + 1, :] + 1.0, (COLS, COLS)))
                bandb[at, :] = jnp.transpose(jnp.broadcast_to(band[i:i + 1, :], (COLS, COLS)))
    for w in weights:
        w.wait()

    order = (2, 3, 4, 5, 0, 1, 6, 7)

    def sources(j):
        others(lambda d: arrival(j, d).wait_recv())
        own(j).wait()

        def prepare(i, total):
            at = pl.ds(pl.multiple_of(i * LB, LB), LB)
            field = got[j, at, :]
            state[at, :] = field.astype(jnp.bfloat16)
            square[at, :] = (field * field).astype(jnp.bfloat16)
            return total + jnp.sum((bandb[at, :] * field).reshape(LB // 8, 8, COLS), axis=0)
        energy = jnp.sum(lax.fori_loop(0, PEERS, prepare, jnp.zeros((8, COLS), jnp.float32)), axis=0, keepdims=True)
        damp = 1.0 / (1.0 + 0.5 * energy)

        def owner(i, carry):
            d = lax.rem(me + i, PEERS)
            at = pl.ds(pl.multiple_of(d * LB, LB), LB)
            gain = jnp.dot(kgv[at, :], state[...], preferred_element_type=jnp.float32)
            loss = jnp.dot(klv[at, :], square[...], preferred_element_type=jnp.float32)
            field = got[j, at, :]
            fresh[j, at, :] = (field * (growb[at, :] + 0.25 * gain) - 0.25 * loss) * damp

            @pl.when(i < PEERS)
            def _():
                give(j, d).start()
            return carry
        lax.fori_loop(1, PEERS + 1, owner, 0)
        keep(j).start()

    for j in order:
        sources(j)

    def save(j):
        return pltpu.make_async_copy(outv.at[:, pl.ds(8 * j, 8), :], out.at[:, pl.ds(8 * j, 8), :], out_sem.at[j])

    for j in order:
        others(lambda d: returned(j, d).wait_recv())
        keep(j).wait()
        sea = mask[8 * j:8 * j + 8, :].astype(jnp.float32)

        def turn(b, carry):
            outv[b, pl.ds(8 * j, 8), :] = back[pl.ds(8 * j * LB + b, 8, stride=LB), :] * sea
            return carry
        lax.fori_loop(0, LB, turn, 0, unroll=8)
        save(j).start()

    for h in halos:
        h.wait_send()
    for j in order:
        others(lambda d: forward(j, d).wait_send())
        others(lambda d: give(j, d).wait_send())
    for j in order:
        save(j).wait()


def local(spectra, land_mask, growth, band_weight, kernel_gain, kernel_loss):
    theta = 2.0 * math.pi * (np.arange(LB) % ND + 0.5) / ND
    wide = lambda v: jnp.asarray(np.repeat(v.astype(np.float32)[:, None], COLS, 1))
    vmem = pl.BlockSpec(memory_space=pltpu.VMEM)
    anym = pl.BlockSpec(memory_space=pl.ANY)
    f32, bf16 = jnp.float32, jnp.bfloat16
    dma = pltpu.SemaphoreType.DMA
    return pl.pallas_call(
        kernel,
        out_shape=jax.ShapeDtypeStruct((LB, ROWS, COLS), f32),
        in_specs=[anym, vmem, vmem, vmem, vmem, vmem, anym, anym],
        out_specs=anym,
        scratch_shapes=[
            pltpu.VMEM((LB, PAD, COLS), f32),
            pltpu.VMEM((PAD, 8, COLS), f32),
            pltpu.VMEM((8, COLS), jnp.int32),
            pltpu.VMEM((8, COLS), jnp.int32),
            pltpu.VMEM((ROWS, LB, COLS), f32),
            pltpu.VMEM((ROUNDS, NB, COLS), f32),
            pltpu.VMEM((ROUNDS, NB, COLS), f32),
            pltpu.VMEM((ROWS * LB, COLS), f32),
            pltpu.VMEM((LB, ROWS, COLS), f32),
            pltpu.VMEM((NB, NB), bf16),
            pltpu.VMEM((NB, NB), bf16),
            pltpu.VMEM((NB, COLS), f32),
            pltpu.VMEM((NB, COLS), f32),
            pltpu.VMEM((NB, COLS), bf16),
            pltpu.VMEM((NB, COLS), bf16),
            dma((10,)), dma((4,)), dma((4,)), dma((2, ROUNDS)),
            dma((ROUNDS, PEERS)), dma((ROUNDS, PEERS)), dma((ROUNDS, PEERS)), dma((ROUNDS, PEERS)),
            dma((ROUNDS,)),
        ],
        compiler_params=pltpu.CompilerParams(collective_id=0, has_side_effects=True, vmem_limit_bytes=56 * 2**20),
    )(spectra, land_mask, wide(np.cos(theta)), wide(np.sin(theta)),
      growth.reshape(NB // COLS, COLS), band_weight.reshape(NB // COLS, COLS), kernel_gain, kernel_loss)


def solution(mesh):
    in_specs = (P("bins", "space", None), P("space", None), P(), P(), P(), P())
    out_specs = P("bins", "space", None)
    return jax.shard_map(local, mesh=mesh, in_specs=in_specs, out_specs=out_specs, check_vma=False)
```

time: 233 us -> 125 us (0.54); the launches traced: 228 us -> 125 us
  Pallas kernels: 0 us -> 120 us
  waiting for transfers between devices: 61.9 us -> 0 us
  blocking collectives: 59.5 us -> 0 us
  other arithmetic: 36.6 us -> 0 us
  local copies, waits for them, and re-layouts: 37.6 us -> 5.24 us
  starting transfers between devices: 18.3 us -> 0 us
  matrix products: 14.3 us -> 0 us
    pallas_call x0 -> x1, Pallas kernels: none -> 120 us  [local(): pl.pallas_call(kernel, out_shape=jax.ShapeDtypeStruct((LB, ROWS, COLS), f...]
    all_to_all x1 -> x0, blocking collectives: 59.5 us -> none  [local(): lax.all_to_all(fresh, 'bins', split_axis=0, concat_axis=1, tiled=True)]
    all_to_all x1 -> x0, waiting for transfers between devices: 54.5 us -> none  [local(): lax.all_to_all(flat, 'bins', split_axis=1, concat_axis=0, tiled=True)]
    all_to_all x4 -> x0, local copies, waits for them, and re-layouts: 24.2 us -> none  [the longest x3 19.2 us: local(): lax.all_to_all(flat, 'bins', split_axis=1, concat_axis=0, tiled=True)]
    mul x5 -> x0, other arithmetic: 21.9 us -> none  [the longest x4 16.4 us: local(): padded = sea_wide[None] * along_columns(padded, speed_y)]
    dot_general x2 -> x0, matrix products: 14.3 us -> none  [the longest x1 8.64 us: sources(): gain = jnp.dot(kernel_gain, state, preferred_element_type=jnp.float32)]
    ppermute x4 -> x0, starting transfers between devices: 11.2 us -> none  [the longest x2 8.64 us: extended(): lax.ppermute(tail, axis, [(i, (i + 1) % count) for i in range(ends)])]
    sub x4 -> x0, other arithmetic: 7.89 us -> none  [along_rows(): middle - plus * (middle - padded[:, :-2]) - minus * (middle - padded[:, 2:])]
  transfers between devices with their start and end apart: 5 -> 0, of which waited for: 3 -> 0; matrix products, arithmetic and copies ran while one was open for 1% -> 0% of each run, Pallas kernels for 0% -> 0%
where the time goes in v1:
time: 125 us
  Pallas kernels  120 us (96%)
  local copies, waits for them, and re-layouts  5.24 us (4%)
    pallas_call x1, Pallas kernels, local(): pl.pallas_call(kernel, out_shape=jax.ShapeDtypeStruct((LB, ROWS, COLS), f...  120 us
    unnamed x1, local copies, waits for them, and re-layouts  5.24 us

profile of v1, /device:TPU:1, one launch (start us, length us, event | category | flops | bytes accessed | tf_op | source)
XLA Modules:
  0.0 124.8 jit_solution(7538127305252237688)
XLA Ops:
  0.0 119.5 %shard_map.82 = f32[144,64,128]{2,1,0:T(8,128)} custom-call(f32[144,64,128]{2,1,0:T(8,128)} %x.1, s32[64,128]{1,0:T(8,128)} %mask.1, f32[144,128]{1,0:T(8,128)} %constant.4.clone.cosv, f32[144,128]{1,0:T(8,128)} %constant.5.clone.sinv, f32[9,128]{1,0:T(8,128)} %bitcast.2, f32[9,128]{1,0:T(8,128)} %bitcast.3, bf16[1152,1152]{1,0:T(8,128)(2,1)} %kg.1, ...), custom_call_target="tpu_custom_call" | custom-call | tf_op jit(solution)/shard_map/pallas_call | solution.py:236
  119.5 5.2 %copy.10 = f32[144,64,128]{2,1,0:T(8,128)} copy(f32[144,64,128]{2,1,0:T(8,128)} %shard_map.82) | data formatting | bytes 9437184

commit v2 on v1

--- a/solution.py
+++ b/solution.py
@@ -31,7 +31,28 @@
     return device // 2 + 4 * lax.rem(device, 2)
 
 
-def kernel(x, mask, cosv, sinv, grow, band, kg, kl, out,
+def advance(field, b0, me, cosv, sinv, lane, sub, sea):
+    b = sub + b0
+    one = lambda c: c.astype(jnp.float32)
+    freq = (4 * me).astype(jnp.float32) + one(b >= ND) + one(b >= 2 * ND) + one(b >= 3 * ND)
+    group = 0.9 / (1.0 + 2.3 * freq / max(NF - 1, 1))
+    cx = group * cosv[pl.ds(b0, 8), :]
+    cy = group * sinv[pl.ds(b0, 8), :]
+    right, ahead = cx > 0.0, cy > 0.0
+    ax, ay = jnp.abs(cx), jnp.abs(cy)
+    stay = 1.0 - ay
+    move = jnp.where((ahead & (lane == 0)) | (~ahead & (lane == COLS - 1)), 0.0, ay)
+    for step in range(SUBSTEPS):
+        n = field.shape[0] - 2
+        mid = field[1:-1]
+        near = jnp.where(right[None], field[:-2], field[2:])
+        mid = mid + ax[None] * (near - mid)
+        near = jnp.stack([jnp.where(ahead, pltpu.roll(mid[i], 1, 1), pltpu.roll(mid[i], COLS - 1, 1)) for i in range(n)])
+        field = (stay[None] * mid + move[None] * near) * sea(step, n)
+    return field
+
+
+def whole_kernel(x, mask, cosv, sinv, grow, band, kg, kl, out,
            fin, seab, mlo, mhi, sent, got, fresh, back, outv, kgv, klv, growb, bandb, state, square,
            load_sem, halo_send, halo_recv, own_sem, fs, fr, bs, br, out_sem):
     me = lax.axis_index("bins")
@@ -82,26 +103,10 @@
             if g == 3:
                 rows = rows[:20] + [r * inside_hi for r in rows[20:]]
             field = jnp.stack(rows)
-            b = sub + b0
-            one = lambda c: c.astype(jnp.float32)
-            freq = (4 * me).astype(jnp.float32) + one(b >= ND) + one(b >= 2 * ND) + one(b >= 3 * ND)
-            group = 0.9 / (1.0 + 2.3 * freq / max(NF - 1, 1))
-            cx = group * cosv[pl.ds(b0, 8), :]
-            cy = group * sinv[pl.ds(b0, 8), :]
-            right, ahead = cx > 0.0, cy > 0.0
-            ax, ay = jnp.abs(cx), jnp.abs(cy)
-            stay = 1.0 - ay
-            move = jnp.where((ahead & (lane == 0)) | (~ahead & (lane == COLS - 1)), 0.0, ay)
-            for step in range(SUBSTEPS):
-                n = field.shape[0] - 2
-                mid = field[1:-1]
-                near = jnp.where(right[None], field[:-2], field[2:])
-                mid = mid + ax[None] * (near - mid)
-                near = jnp.stack([jnp.where(ahead, pltpu.roll(mid[i], 1, 1), pltpu.roll(mid[i], COLS - 1, 1)) for i in range(n)])
-                field = (stay[None] * mid + move[None] * near) * seab[pl.ds(16 * g + 5 + step, n)]
+            field = advance(field, b0, me, cosv, sinv, lane, sub, lambda step, n: seab[pl.ds(16 * g + 5 + step, n)])
             sent[pl.ds(16 * g, 16), pl.ds(b0, 8), :] = field
             return carry
-        lax.fori_loop(0, LB // 8, tile, 0)
+        lax.fori_loop(0, LB // 8, tile, 0, unroll=2)
 
     def forward(j, d):
         row = 8 * j + slot_of(d)
@@ -226,41 +231,412 @@
         save(j).wait()
 
 
+ORDER = (1, 2, 0, 3)
+BASE = 13
+EXT = 3
+TILES = BASE * 4
+CAP = BASE * COLS
+
+
+def sea_kernel(x, mask, cosv, sinv, grow, band, kg, kl, out, flag,
+               fin, seab, mlo, mhi, sent, extra, halves, place, hole_at, got, fresh, back, total, outv,
+               kgv, klv, growb, bandb, state, square, flx, flz,
+               load_sem, halo_send, halo_recv, fs, fr, bs, br, out_sem, fls, flr):
+    me = lax.axis_index("bins")
+    space = lax.axis_index("space")
+    up = lax.rem(space + 1, SLABS)
+    down = lax.rem(space + SLABS - 1, SLABS)
+    core = lax.rem(me, 2)
+    mine = slot_of(me)
+    sx = lax.rem(space, 4)
+    sz = space // 4
+    f32, bf16 = jnp.float32, jnp.bfloat16
+
+    def x_peer(i):
+        return sz * 4 + lax.rem(sx + i, 4)
+
+    def z_peer(i):
+        return lax.rem(sz + i, 4) * 4 + sx
+
+    barrier = pltpu.get_barrier_semaphore()
+    for i in range(1, PEERS):
+        pl.semaphore_signal(barrier, inc=1, device_id=(lax.rem(me + i, PEERS), space), device_id_type=MESH)
+    for other in [up, down] + [x_peer(i) for i in (1, 2, 3)] + [z_peer(i) for i in (1, 2, 3)]:
+        pl.semaphore_signal(barrier, inc=1, device_id=(me, other), device_id_type=MESH)
+
+    def load(q):
+        return pltpu.make_async_copy(x.at[:, pl.ds(8 * q, 8), :], fin.at[:, pl.ds(8 * q + 8, 8), :], load_sem.at[q])
+
+    for q in (1, 2, 3, 4, 5, 6, 0, 7):
+        load(q).start()
+    weights = [pltpu.make_async_copy(kg, kgv, load_sem.at[8]), pltpu.make_async_copy(kl, klv, load_sem.at[9])]
+
+    for q in range(ROWS // 8):
+        sea = mask[8 * q:8 * q + 8, :].astype(f32)
+        for i in range(8):
+            seab[8 + 8 * q + i] = jnp.broadcast_to(sea[i:i + 1, :], (8, COLS))
+
+    halos = [
+        pltpu.make_async_remote_copy(x.at[:, pl.ds(56, 8), :], fin.at[:, pl.ds(0, 8), :], halo_send.at[0], halo_recv.at[0],
+                                     device_id=(me, up), device_id_type=MESH),
+        pltpu.make_async_remote_copy(x.at[:, pl.ds(0, 8), :], fin.at[:, pl.ds(72, 8), :], halo_send.at[1], halo_recv.at[1],
+                                     device_id=(me, down), device_id_type=MESH),
+        pltpu.make_async_remote_copy(mask.at[pl.ds(56, 8), :], mlo, halo_send.at[2], halo_recv.at[2],
+                                     device_id=(me, up), device_id_type=MESH),
+        pltpu.make_async_remote_copy(mask.at[pl.ds(0, 8), :], mhi, halo_send.at[3], halo_recv.at[3],
+                                     device_id=(me, down), device_id_type=MESH),
+    ]
+    inside_lo = (space > 0).astype(f32)
+    inside_hi = (space < SLABS - 1).astype(f32)
+    flat = fin.reshape(LB * PAD, COLS)
+    lane = lax.broadcasted_iota(jnp.int32, (8, COLS), 1)
+    sub = lax.broadcasted_iota(jnp.int32, (8, COLS), 0)
+
+    before = (lax.broadcasted_iota(jnp.int32, (COLS, COLS), 0) < lax.broadcasted_iota(jnp.int32, (COLS, COLS), 1)).astype(f32).astype(bf16)
+    ones = jnp.ones((COLS, COLS), bf16)
+
+    def assign(p):
+        g = ORDER[p]
+        sea = mask[16 * g:16 * g + 16, :].astype(f32)
+        row = lax.broadcasted_iota(jnp.int32, (16, COLS), 0)
+        pick = jnp.where(row < BASE, 1.0 - sea, sea)
+        ranks = jnp.dot(pick.astype(bf16), before, preferred_element_type=f32)
+        counts = jnp.dot(pick.astype(bf16), ones, preferred_element_type=f32)
+        holes = jnp.zeros((1, COLS), f32)
+        for i in range(BASE):
+            hole_at[i:i + 1, :] = jnp.where(pick[i:i + 1] > 0.0, ranks[i:i + 1] + holes, -1.0)
+            holes = holes + counts[i:i + 1]
+        filled = jnp.zeros((1, COLS), f32)
+        wants = []
+        for i in range(BASE, 16):
+            want = jnp.where(pick[i:i + 1] > 0.0, ranks[i:i + 1] + filled, -2.0)
+            wants.append(jnp.transpose(jnp.broadcast_to(want, (COLS, COLS))))
+            filled = filled + counts[i:i + 1]
+
+        def one(i, carry):
+            hole = hole_at[pl.ds(i, 1), :]
+            for k in range(EXT):
+                place[BASE * p + i, k * COLS:(k + 1) * COLS, :] = jnp.where(wants[k] == hole, 1.0, 0.0).astype(bf16)
+            return carry
+        lax.fori_loop(0, BASE, one, 0)
+        return filled - holes
+
+    def propagate(p):
+        g = ORDER[p]
+
+        def tile(t, carry):
+            b0 = pl.multiple_of(t * 8, 8)
+            rows = [flat[pl.ds(b0 * PAD + 16 * g + 4 + i, 8, stride=PAD), :] for i in range(24)]
+            if g == 0:
+                rows = [r * inside_lo for r in rows[:4]] + rows[4:]
+            if g == 3:
+                rows = rows[:20] + [r * inside_hi for r in rows[20:]]
+            field = advance(jnp.stack(rows), b0, me, cosv, sinv, lane, sub, lambda step, n: seab[pl.ds(16 * g + 5 + step, n)])
+            sent[pl.ds(BASE * p, BASE), pl.ds(b0, 8), :] = field[:BASE]
+            extra[:, pl.ds(b0, 8), :] = field[BASE:]
+            return carry
+        lax.fori_loop(0, LB // 8, tile, 0, unroll=2)
+        for k in range(EXT):
+            cells = extra[k]
+            high = cells.astype(bf16)
+            halves[0:LB, k * COLS:(k + 1) * COLS] = high
+            halves[LB:2 * LB, k * COLS:(k + 1) * COLS] = (cells - high.astype(f32)).astype(bf16)
+
+    def forward(q):
+        d = device_of(lax.rem(q, 8))
+        return d, pltpu.make_async_remote_copy(
+            sent.at[q], got.at[q // 8, pl.ds(me * LB, LB), :], fs.at[q], fr.at[q // 8, me],
+            device_id=(d, space), device_id_type=MESH)
+
+    def arrival(j, d):
+        return pltpu.make_async_remote_copy(
+            sent.at[0], got.at[j, pl.ds(d * LB, LB), :], fs.at[0], fr.at[j, d],
+            device_id=(lax.rem(me + 1, PEERS), space), device_id_type=MESH)
+
+    def seat(q):
+        return ((q // BASE) * 16 + lax.rem(q, BASE)) * LB
+
+    def give(j, d):
+        return pltpu.make_async_remote_copy(
+            fresh.at[j, pl.ds(d * LB, LB), :], back.at[pl.ds(seat(8 * j + mine), LB), :], bs.at[j, d], br.at[8 * j + mine],
+            device_id=(d, space), device_id_type=MESH)
+
+    def returned(q):
+        return pltpu.make_async_remote_copy(
+            fresh.at[0, pl.ds(0, LB), :], back.at[pl.ds(seat(q), LB), :], bs.at[0, 0], br.at[q],
+            device_id=(lax.rem(me + 1, PEERS), space), device_id_type=MESH)
+
+    def fill_and_send(p):
+        def one(i, carry):
+            q = BASE * p + i
+            moved = jnp.dot(halves[...], place[q], preferred_element_type=f32)
+            sent[q] = sent[q] + (moved[:LB] + moved[LB:])
+            d, copy = forward(q)
+
+            @pl.when(d != me)
+            def _():
+                copy.start()
+
+            @pl.when(d == me)
+            def _():
+                pltpu.make_async_copy(sent.at[q], got.at[q // 8, pl.ds(me * LB, LB), :], fr.at[q // 8, me]).start()
+            return carry
+        lax.fori_loop(0, BASE, one, 0)
+
+    ready = set()
+    over = assign(0)
+    for p, g in enumerate(ORDER):
+        for q in range(max(2 * g - 1, 0), min(2 * g + 3, 8)):
+            if q not in ready:
+                load(q).wait()
+                ready.add(q)
+        if p == 2:
+            for h in halos:
+                h.wait_recv()
+            for q, (ref, inside) in ((0, (mlo, inside_lo)), (72, (mhi, inside_hi))):
+                sea = ref[...].astype(f32) * inside
+                for i in range(8):
+                    seab[q + i] = jnp.broadcast_to(sea[i:i + 1, :], (8, COLS))
+        propagate(p)
+        if p == 0:
+            pl.semaphore_wait(barrier, PEERS + 7)
+            for h in halos:
+                h.start()
+        fill_and_send(p)
+        if p < 3:
+            over = jnp.maximum(over, assign(p + 1))
+        if p == 1:
+            for w in weights:
+                w.start()
+            for i in range(NB // COLS):
+                at = pl.ds(i * COLS, COLS)
+                growb[at, :] = jnp.transpose(jnp.broadcast_to(0.25 * grow[i:i + 1, :] + 1.0, (COLS, COLS)))
+                bandb[at, :] = jnp.transpose(jnp.broadcast_to(band[i:i + 1, :], (COLS, COLS)))
+
+    def tell(stage, i):
+        ref, at, to = ((flx, sx, x_peer(i)), (flz, sz, z_peer(i)))[stage]
+        return pltpu.make_async_remote_copy(ref.at[at], ref.at[at], fls.at[stage, i], flr.at[stage, at],
+                                            device_id=(me, to), device_id_type=MESH)
+
+    def told(stage, i):
+        ref, at, to = ((flx, sx, x_peer(i)), (flz, sz, z_peer(i)))[stage]
+        at = lax.rem(at + i, 4)
+        return pltpu.make_async_remote_copy(ref.at[at], ref.at[at], fls.at[stage, i], flr.at[stage, at],
+                                            device_id=(me, to), device_id_type=MESH)
+
+    flx[sx] = jnp.broadcast_to(over, (8, COLS))
+    for i in (1, 2, 3):
+        tell(0, i).start()
+    for w in weights:
+        w.wait()
+
+    def sources(j):
+        def each(d, carry):
+            arrival(j, d).wait_recv()
+            return carry
+        lax.fori_loop(0, PEERS, each, 0)
+
+        def prepare(i, total):
+            at = pl.ds(pl.multiple_of(i * LB, LB), LB)
+            field = got[j, at, :]
+            state[at, :] = field.astype(bf16)
+            square[at, :] = (field * field).astype(bf16)
+            return total + jnp.sum((bandb[at, :] * field).reshape(LB // 8, 8, COLS), axis=0)
+        energy = jnp.sum(lax.fori_loop(0, PEERS, prepare, jnp.zeros((8, COLS), f32)), axis=0, keepdims=True)
+        damp = 1.0 / (1.0 + 0.5 * energy)
+
+        def owner(i, carry):
+            d = lax.rem(me + i, PEERS)
+            at = pl.ds(pl.multiple_of(d * LB, LB), LB)
+            gain = jnp.dot(kgv[at, :], state[...], preferred_element_type=f32)
+            loss = jnp.dot(klv[at, :], square[...], preferred_element_type=f32)
+            field = got[j, at, :]
+            fresh[j, at, :] = (field * (growb[at, :] + 0.25 * gain) - 0.25 * loss) * damp
+
+            @pl.when(i < PEERS)
+            def _():
+                give(j, d).start()
+            return carry
+        lax.fori_loop(1, PEERS + 1, owner, 0)
+        pltpu.make_async_copy(
+            fresh.at[j, pl.ds(me * LB, LB), :], back.at[pl.ds(seat(8 * j + mine), LB), :], br.at[8 * j + mine]).start()
+
+    def full_rounds(j, carry):
+        sources(j)
+        return carry
+    lax.fori_loop(0, 6, full_rounds, 0)
+
+    @pl.when(core == 0)
+    def _():
+        sources(6)
+
+    for i in (1, 2, 3):
+        told(0, i).wait_recv()
+    flz[sz] = jnp.maximum(jnp.maximum(flx[0], flx[1]), jnp.maximum(flx[2], flx[3]))
+    for i in (1, 2, 3):
+        tell(1, i).start()
+
+    def save(q):
+        return pltpu.make_async_copy(outv.at[:, pl.ds(8 * q, 8), :], out.at[:, pl.ds(8 * q, 8), :], out_sem.at[q])
+
+    for p, g in enumerate(ORDER):
+        total[...] = jnp.zeros_like(total)
+
+        def pull(i, carry):
+            q = BASE * p + i
+            returned(q).wait_recv()
+            cells = back[pl.ds(pl.multiple_of((16 * p + i) * LB, LB), LB), :]
+            high = cells.astype(bf16)
+            low = (cells - high.astype(f32)).astype(bf16)
+            both = jnp.concatenate([high, low], axis=0)
+            total[...] += lax.dot_general(both, place[q], (((1,), (1,)), ((), ())), preferred_element_type=f32)
+            return carry
+        lax.fori_loop(0, BASE, pull, 0)
+        for k in range(EXT):
+            at = slice(k * COLS, (k + 1) * COLS)
+            back[pl.ds((16 * p + BASE + k) * LB, LB), :] = total[:LB, at] + total[LB:, at]
+        for h in (0, 1):
+            r0 = 16 * g + 8 * h
+            sea = mask[r0:r0 + 8, :].astype(f32)
+
+            def turn(b, carry):
+                outv[b, pl.ds(r0, 8), :] = back[pl.ds((16 * p + 8 * h) * LB + b, 8, stride=LB), :] * sea
+                return carry
+            lax.fori_loop(0, LB, turn, 0, unroll=8)
+            save(2 * g + h).start()
+
+    for i in (1, 2, 3):
+        told(1, i).wait_recv()
+    flag[...] = jnp.maximum(jnp.maximum(flz[0], flz[1]), jnp.maximum(flz[2], flz[3]))
+    for h in halos:
+        h.wait_send()
+    for i in (1, 2, 3):
+        tell(0, i).wait_send()
+        tell(1, i).wait_send()
+
+    def drain(q, carry):
+        d, copy = forward(q)
+
+        @pl.when(d != me)
+        def _():
+            copy.wait_send()
+        return carry
+    lax.fori_loop(0, TILES, drain, 0)
+
+    def drain_round(j):
+        def step(i, carry):
+            give(j, lax.rem(me + i, PEERS)).wait_send()
+            return carry
+        lax.fori_loop(1, PEERS, step, 0)
+
+    for j in range(6):
+        drain_round(j)
+
+    @pl.when(core == 0)
+    def _():
+        drain_round(6)
+    for q in range(8):
+        save(q).wait()
+
+
+def finish_kernel(packed, out, staged, load_sem, save_sem):
+    part = LB // 12
+    loads, saves = [], []
+    for i in range(12):
+        at = pl.ds(i * part, part)
+        loads.append(pltpu.make_async_copy(packed.at[at], staged.at[at], load_sem.at[i]))
+        saves.append(pltpu.make_async_copy(staged.at[at], out.at[at], save_sem.at[i]))
+    for load in loads:
+        load.start()
+    for load, save in zip(loads, saves):
+        load.wait()
+        save.start()
+    for save in saves:
+        save.wait()
+
+
 def local(spectra, land_mask, growth, band_weight, kernel_gain, kernel_loss):
     theta = 2.0 * math.pi * (np.arange(LB) % ND + 0.5) / ND
     wide = lambda v: jnp.asarray(np.repeat(v.astype(np.float32)[:, None], COLS, 1))
     vmem = pl.BlockSpec(memory_space=pltpu.VMEM)
     anym = pl.BlockSpec(memory_space=pl.ANY)
-    f32, bf16 = jnp.float32, jnp.bfloat16
+    f32, bf16, i32 = jnp.float32, jnp.bfloat16, jnp.int32
     dma = pltpu.SemaphoreType.DMA
-    return pl.pallas_call(
-        kernel,
-        out_shape=jax.ShapeDtypeStruct((LB, ROWS, COLS), f32),
-        in_specs=[anym, vmem, vmem, vmem, vmem, vmem, anym, anym],
-        out_specs=anym,
-        scratch_shapes=[
-            pltpu.VMEM((LB, PAD, COLS), f32),
-            pltpu.VMEM((PAD, 8, COLS), f32),
-            pltpu.VMEM((8, COLS), jnp.int32),
-            pltpu.VMEM((8, COLS), jnp.int32),
-            pltpu.VMEM((ROWS, LB, COLS), f32),
-            pltpu.VMEM((ROUNDS, NB, COLS), f32),
-            pltpu.VMEM((ROUNDS, NB, COLS), f32),
+    shape = jax.ShapeDtypeStruct((LB, ROWS, COLS), f32)
+    operands = (spectra, land_mask, wide(np.cos(theta)), wide(np.sin(theta)),
+                growth.reshape(NB // COLS, COLS), band_weight.reshape(NB // COLS, COLS), kernel_gain, kernel_loss)
+    in_specs = [anym, vmem, vmem, vmem, vmem, vmem, anym, anym]
+    weights = [
+        pltpu.VMEM((NB, NB), bf16),
+        pltpu.VMEM((NB, NB), bf16),
+        pltpu.VMEM((NB, COLS), f32),
+        pltpu.VMEM((NB, COLS), f32),
+        pltpu.VMEM((NB, COLS), bf16),
+        pltpu.VMEM((NB, COLS), bf16),
+    ]
+    edges = [
+        pltpu.VMEM((LB, PAD, COLS), f32),
+        pltpu.VMEM((PAD, 8, COLS), f32),
+        pltpu.VMEM((8, COLS), i32),
+        pltpu.VMEM((8, COLS), i32),
+    ]
+
+    def finish(packed):
+        return pl.pallas_call(
+            finish_kernel,
+            out_shape=shape,
+            in_specs=[anym],
+            out_specs=anym,
+            scratch_shapes=[pltpu.VMEM((LB, ROWS, COLS), f32), dma((12,)), dma((12,))],
+            compiler_params=pltpu.CompilerParams(vmem_limit_bytes=62 * 2**20),
+        )(packed)
+
+    def whole(args):
+        return finish(pl.pallas_call(
+            whole_kernel,
+            out_shape=shape,
+            in_specs=in_specs,
+            out_specs=anym,
+            scratch_shapes=edges + [
+                pltpu.VMEM((ROWS, LB, COLS), f32),
+                pltpu.VMEM((ROUNDS, NB, COLS), f32),
+                pltpu.VMEM((ROUNDS, NB, COLS), f32),
+                pltpu.VMEM((ROWS * LB, COLS), f32),
+                pltpu.VMEM((LB, ROWS, COLS), f32),
+            ] + weights + [
+                dma((10,)), dma((4,)), dma((4,)), dma((2, ROUNDS)),
+                dma((ROUNDS, PEERS)), dma((ROUNDS, PEERS)), dma((ROUNDS, PEERS)), dma((ROUNDS, PEERS)),
+                dma((ROUNDS,)),
+            ],
+            compiler_params=pltpu.CompilerParams(collective_id=1, has_side_effects=True, vmem_limit_bytes=62 * 2**20),
+        )(*args[1:]))
+
+    packed, flag = pl.pallas_call(
+        sea_kernel,
+        out_shape=(shape, pltpu.VMEM((8, COLS), f32)),
+        in_specs=in_specs,
+        out_specs=(anym, vmem),
+        scratch_shapes=edges + [
+            pltpu.VMEM((TILES, LB, COLS), f32),
+            pltpu.VMEM((EXT, LB, COLS), f32),
+            pltpu.VMEM((2 * LB, EXT * COLS), bf16),
+            pltpu.VMEM((TILES, EXT * COLS, COLS), bf16),
+            pltpu.VMEM((16, COLS), f32),
+            pltpu.VMEM((7, NB, COLS), f32),
+            pltpu.VMEM((7, NB, COLS), f32),
             pltpu.VMEM((ROWS * LB, COLS), f32),
+            pltpu.VMEM((2 * LB, EXT * COLS), f32),
             pltpu.VMEM((LB, ROWS, COLS), f32),
-            pltpu.VMEM((NB, NB), bf16),
-            pltpu.VMEM((NB, NB), bf16),
-            pltpu.VMEM((NB, COLS), f32),
-            pltpu.VMEM((NB, COLS), f32),
-            pltpu.VMEM((NB, COLS), bf16),
-            pltpu.VMEM((NB, COLS), bf16),
-            dma((10,)), dma((4,)), dma((4,)), dma((2, ROUNDS)),
-            dma((ROUNDS, PEERS)), dma((ROUNDS, PEERS)), dma((ROUNDS, PEERS)), dma((ROUNDS, PEERS)),
-            dma((ROUNDS,)),
+        ] + weights + [
+            pltpu.VMEM((4, 8, COLS), f32),
+            pltpu.VMEM((4, 8, COLS), f32),
+            dma((10,)), dma((4,)), dma((4,)),
+            dma((TILES,)), dma((7, PEERS)), dma((7, PEERS)), dma((TILES,)),
+            dma((8,)), dma((2, 4)), dma((2, 4)),
         ],
-        compiler_params=pltpu.CompilerParams(collective_id=0, has_side_effects=True, vmem_limit_bytes=56 * 2**20),
-    )(spectra, land_mask, wide(np.cos(theta)), wide(np.sin(theta)),
-      growth.reshape(NB // COLS, COLS), band_weight.reshape(NB // COLS, COLS), kernel_gain, kernel_loss)
+        compiler_params=pltpu.CompilerParams(collective_id=0, has_side_effects=True, vmem_limit_bytes=62 * 2**20),
+    )(*operands)
+    return lax.cond(flag[0, 0] > 0.0, whole, lambda args: finish(args[0]), (packed,) + operands)
 
 
 def solution(mesh):

time: 125 us -> 109 us (0.87)
  Pallas kernels: 120 us -> 107 us
  local copies, waits for them, and re-layouts: 5.24 us -> 0.53 us
    pallas_call x1 -> x2, Pallas kernels: 120 us -> 107 us  [the longest x1 103 us: local(): pl.pallas_call(sea_kernel, out_shape=(shape, pltpu.VMEM((8, COLS), f32)),...]
    unnamed x1 -> x10, local copies, waits for them, and re-layouts: 5.24 us -> 0.02 us
where the time goes in v2:
time: 109 us; the launch traced here: 108 us
  Pallas kernels  107 us (98%)
    pallas_call x1, Pallas kernels, local(): pl.pallas_call(sea_kernel, out_shape=(shape, pltpu.VMEM((8, COLS), f32)),...  103 us
    pallas_call x1, Pallas kernels, finish(): pl.pallas_call(finish_kernel, out_shape=shape, in_specs=[anym], out_specs...  4.27 us

profile of v2, /device:TPU:1, one launch (start us, length us, event | category | flops | bytes accessed | tf_op | source)
XLA Modules:
  0.0 108.5 jit_solution(4476678259270274207)
XLA Ops:
  0.0 0.0 copy-start
  0.0 0.0 copy-start.1
  0.0 0.0 copy-start.2
  0.0 0.0 copy-start.3
  0.0 0.0 copy-start.4
  0.0 102.9 %shard_map.84 = (f32[144,64,128]{2,1,0:T(8,128)}, f32[8,128]{1,0:T(8,128)S(1)}) custom-call(f32[144,64,128]{2,1,0:T(8,128)} %x.1, s32[64,128]{1,0:T(8,128)} %mask.1, f32[144,128]{1,0:T(8,128)} %constant.7.clone.cosv, f32[144,128]{1,0:T(8,128)} %constant.8.clone.sinv, f32[9,128]{1,0:T(8,128)} %bitcast.3, f32[9,128]{1,0:T(8,128)} %bitcast.5, ...), custom_call_target="tpu_custom_call" | custom-call | tf_op jit(solution)/shard_map/pallas_call | solution.py:614
  103.0 0.5 slice.3
  104.1 0.0 copy-done
  104.1 0.0 copy-done.1
  104.2 0.0 copy-done.2
  104.2 0.0 copy-done.3
  104.2 0.0 copy-done.4
  104.2 4.3 %conditional.1 = (f32[144,64,128]{2,1,0:T(8,128)}) conditional(s32[]{:T(128)} %bitcast.2, f32[144,64,128]{2,1,0:T(8,128)} %get-tuple-element.36, (f32[144,64,128]{2,1,0:T(8,128)}, s32[64,128]{1,0:T(8,128)S(1)}, f32[144,128]{1,0:T(8,128)S(1)}, f32[144,128]{1,0:T(8,128)S(1)}, f32[9,128]{1,0:T(8,128)S(1)}, /*index=5*/f32[9,128]{1,0:T(8,128)S(1)}, ...), branch_computations={%region_0.0_spmd, %region_1.0_spmd} | conditional | bytes 8 | solution.py:639
  104.2 4.3 %branch_0_fun.1 = f32[144,64,128]{2,1,0:T(8,128)} custom-call(f32[144,64,128]{2,1,0:T(8,128)} %packed), custom_call_target="tpu_custom_call" | custom-call | tf_op jit(solution)/shard_map/cond/branch_0_fun/pallas_call | solution.py:585
Async XLA Ops:
  0.0 104.1 %copy-start = (f32[144,128]{1,0:T(8,128)S(1)}, f32[144,128]{1,0:T(8,128)}, u32[]{:S(2)}) copy-start(f32[144,128]{1,0:T(8,128)} %constant.8.clone.sinv) | copy-start | bytes 221188
  0.0 104.1 %copy-start.1 = (f32[144,128]{1,0:T(8,128)S(1)}, f32[144,128]{1,0:T(8,128)}, u32[]{:S(2)}) copy-start(f32[144,128]{1,0:T(8,128)} %constant.7.clone.cosv) | copy-start | bytes 221188
  0.0 104.2 %copy-start.2 = (s32[64,128]{1,0:T(8,128)S(1)}, s32[64,128]{1,0:T(8,128)}, u32[]{:S(2)}) copy-start(s32[64,128]{1,0:T(8,128)} %mask.1) | copy-start | bytes 98308
  0.0 104.2 %copy-start.3 = (f32[1152]{0:T(1024)S(1)}, f32[1152]{0:T(1024)}, u32[]{:S(2)}) copy-start(f32[1152]{0:T(1024)} %param.12) | copy-start | bytes 13828
  0.0 104.2 %copy-start.4 = (f32[1152]{0:T(1024)S(1)}, f32[1152]{0:T(1024)}, u32[]{:S(2)}) copy-start(f32[1152]{0:T(1024)} %param.13) | copy-start | bytes 13828

commit v3 on v2

--- a/solution.py
+++ b/solution.py
@@ -53,8 +53,8 @@
 
 
 def whole_kernel(x, mask, cosv, sinv, grow, band, kg, kl, out,
-           fin, seab, mlo, mhi, sent, got, fresh, back, outv, kgv, klv, growb, bandb, state, square,
-           load_sem, halo_send, halo_recv, own_sem, fs, fr, bs, br, out_sem):
+           fin, seab, mlo, mhi, sent, got, fresh, back, kgv, klv, growb, bandb, state, square,
+           load_sem, halo_send, halo_recv, own_sem, fs, fr, bs, br):
     me = lax.axis_index("bins")
     space = lax.axis_index("space")
     up = lax.rem(space + 1, SLABS)
@@ -208,40 +208,34 @@
     for j in order:
         sources(j)
 
-    def save(j):
-        return pltpu.make_async_copy(outv.at[:, pl.ds(8 * j, 8), :], out.at[:, pl.ds(8 * j, 8), :], out_sem.at[j])
-
     for j in order:
         others(lambda d: returned(j, d).wait_recv())
         keep(j).wait()
         sea = mask[8 * j:8 * j + 8, :].astype(jnp.float32)
 
         def turn(b, carry):
-            outv[b, pl.ds(8 * j, 8), :] = back[pl.ds(8 * j * LB + b, 8, stride=LB), :] * sea
+            out[b, pl.ds(8 * j, 8), :] = back[pl.ds(8 * j * LB + b, 8, stride=LB), :] * sea
             return carry
         lax.fori_loop(0, LB, turn, 0, unroll=8)
-        save(j).start()
 
     for h in halos:
         h.wait_send()
     for j in order:
         others(lambda d: forward(j, d).wait_send())
         others(lambda d: give(j, d).wait_send())
-    for j in order:
-        save(j).wait()
 
 
 ORDER = (1, 2, 0, 3)
 BASE = 13
 EXT = 3
 TILES = BASE * 4
-CAP = BASE * COLS
+SPLIT = 80
 
 
 def sea_kernel(x, mask, cosv, sinv, grow, band, kg, kl, out, flag,
-               fin, seab, mlo, mhi, sent, extra, halves, place, hole_at, got, fresh, back, total, outv,
+               fin, seab, mlo, mhi, sent, extra, halves, place, hole_at, got, fresh, back, total,
                kgv, klv, growb, bandb, state, square, flx, flz,
-               load_sem, halo_send, halo_recv, fs, fr, bs, br, out_sem, fls, flr):
+               load_sem, halo_send, halo_recv, fs, fr, bs, br, fls, flr):
     me = lax.axis_index("bins")
     space = lax.axis_index("space")
     up = lax.rem(space + 1, SLABS)
@@ -321,11 +315,11 @@
         lax.fori_loop(0, BASE, one, 0)
         return filled - holes
 
-    def propagate(p):
+    def propagate(p, lo, hi):
         g = ORDER[p]
 
         def tile(t, carry):
-            b0 = pl.multiple_of(t * 8, 8)
+            b0 = pl.multiple_of(lo + t * 8, 8)
             rows = [flat[pl.ds(b0 * PAD + 16 * g + 4 + i, 8, stride=PAD), :] for i in range(24)]
             if g == 0:
                 rows = [r * inside_lo for r in rows[:4]] + rows[4:]
@@ -335,17 +329,17 @@
             sent[pl.ds(BASE * p, BASE), pl.ds(b0, 8), :] = field[:BASE]
             extra[:, pl.ds(b0, 8), :] = field[BASE:]
             return carry
-        lax.fori_loop(0, LB // 8, tile, 0, unroll=2)
+        lax.fori_loop(0, (hi - lo) // 8, tile, 0, unroll=2)
         for k in range(EXT):
-            cells = extra[k]
+            cells = extra[k, lo:hi, :]
             high = cells.astype(bf16)
-            halves[0:LB, k * COLS:(k + 1) * COLS] = high
-            halves[LB:2 * LB, k * COLS:(k + 1) * COLS] = (cells - high.astype(f32)).astype(bf16)
-
-    def forward(q):
+            halves[2 * lo:lo + hi, k * COLS:(k + 1) * COLS] = high
+            halves[lo + hi:2 * hi, k * COLS:(k + 1) * COLS] = (cells - high.astype(f32)).astype(bf16)
+
+    def forward(q, lo=0, hi=LB):
         d = device_of(lax.rem(q, 8))
         return d, pltpu.make_async_remote_copy(
-            sent.at[q], got.at[q // 8, pl.ds(me * LB, LB), :], fs.at[q], fr.at[q // 8, me],
+            sent.at[q, pl.ds(lo, hi - lo), :], got.at[q // 8, pl.ds(me * LB + lo, hi - lo), :], fs.at[q], fr.at[q // 8, me],
             device_id=(d, space), device_id_type=MESH)
 
     def arrival(j, d):
@@ -366,12 +360,15 @@
             fresh.at[0, pl.ds(0, LB), :], back.at[pl.ds(seat(q), LB), :], bs.at[0, 0], br.at[q],
             device_id=(lax.rem(me + 1, PEERS), space), device_id_type=MESH)
 
-    def fill_and_send(p):
+    def fill_and_send(p, lo, hi):
+        n = hi - lo
+        at = pl.ds(lo, n)
+
         def one(i, carry):
             q = BASE * p + i
-            moved = jnp.dot(halves[...], place[q], preferred_element_type=f32)
-            sent[q] = sent[q] + (moved[:LB] + moved[LB:])
-            d, copy = forward(q)
+            moved = jnp.dot(halves[2 * lo:2 * hi, :], place[q], preferred_element_type=f32)
+            sent[q, at, :] = sent[q, at, :] + (moved[:n] + moved[n:])
+            d, copy = forward(q, lo, hi)
 
             @pl.when(d != me)
             def _():
@@ -379,7 +376,7 @@
 
             @pl.when(d == me)
             def _():
-                pltpu.make_async_copy(sent.at[q], got.at[q // 8, pl.ds(me * LB, LB), :], fr.at[q // 8, me]).start()
+                pltpu.make_async_copy(sent.at[q, at, :], got.at[q // 8, pl.ds(me * LB + lo, n), :], fr.at[q // 8, me]).start()
             return carry
         lax.fori_loop(0, BASE, one, 0)
 
@@ -397,12 +394,13 @@
                 sea = ref[...].astype(f32) * inside
                 for i in range(8):
                     seab[q + i] = jnp.broadcast_to(sea[i:i + 1, :], (8, COLS))
-        propagate(p)
-        if p == 0:
-            pl.semaphore_wait(barrier, PEERS + 7)
-            for h in halos:
-                h.start()
-        fill_and_send(p)
+        for lo, hi in ((0, SPLIT), (SPLIT, LB)) if p == 0 else ((0, LB),):
+            propagate(p, lo, hi)
+            if p == 0 and lo == 0:
+                pl.semaphore_wait(barrier, PEERS + 7)
+                for h in halos:
+                    h.start()
+            fill_and_send(p, lo, hi)
         if p < 3:
             over = jnp.maximum(over, assign(p + 1))
         if p == 1:
@@ -476,9 +474,6 @@
     for i in (1, 2, 3):
         tell(1, i).start()
 
-    def save(q):
-        return pltpu.make_async_copy(outv.at[:, pl.ds(8 * q, 8), :], out.at[:, pl.ds(8 * q, 8), :], out_sem.at[q])
-
     for p, g in enumerate(ORDER):
         total[...] = jnp.zeros_like(total)
 
@@ -500,10 +495,9 @@
             sea = mask[r0:r0 + 8, :].astype(f32)
 
             def turn(b, carry):
-                outv[b, pl.ds(r0, 8), :] = back[pl.ds((16 * p + 8 * h) * LB + b, 8, stride=LB), :] * sea
+                out[b, pl.ds(r0, 8), :] = back[pl.ds((16 * p + 8 * h) * LB + b, 8, stride=LB), :] * sea
                 return carry
             lax.fori_loop(0, LB, turn, 0, unroll=8)
-            save(2 * g + h).start()
 
     for i in (1, 2, 3):
         told(1, i).wait_recv()
@@ -535,24 +529,15 @@
     @pl.when(core == 0)
     def _():
         drain_round(6)
-    for q in range(8):
-        save(q).wait()
-
-
-def finish_kernel(packed, out, staged, load_sem, save_sem):
-    part = LB // 12
-    loads, saves = [], []
-    for i in range(12):
-        at = pl.ds(i * part, part)
-        loads.append(pltpu.make_async_copy(packed.at[at], staged.at[at], load_sem.at[i]))
-        saves.append(pltpu.make_async_copy(staged.at[at], out.at[at], save_sem.at[i]))
-    for load in loads:
-        load.start()
-    for load, save in zip(loads, saves):
-        load.wait()
-        save.start()
-    for save in saves:
-        save.wait()
+
+
+def finish_kernel(packed, out, sems):
+    part = LB // 8
+    copies = [pltpu.make_async_copy(packed.at[pl.ds(i * part, part)], out.at[pl.ds(i * part, part)], sems.at[i]) for i in range(8)]
+    for copy in copies:
+        copy.start()
+    for copy in copies:
+        copy.wait()
 
 
 def local(spectra, land_mask, growth, band_weight, kernel_gain, kernel_loss):
@@ -585,37 +570,35 @@
         return pl.pallas_call(
             finish_kernel,
             out_shape=shape,
-            in_specs=[anym],
+            in_specs=[vmem],
             out_specs=anym,
-            scratch_shapes=[pltpu.VMEM((LB, ROWS, COLS), f32), dma((12,)), dma((12,))],
-            compiler_params=pltpu.CompilerParams(vmem_limit_bytes=62 * 2**20),
+            scratch_shapes=[dma((8,))],
+            compiler_params=pltpu.CompilerParams(vmem_limit_bytes=16 * 2**20),
         )(packed)
 
     def whole(args):
-        return finish(pl.pallas_call(
+        return (pl.pallas_call(
             whole_kernel,
-            out_shape=shape,
+            out_shape=pltpu.VMEM((LB, ROWS, COLS), f32),
             in_specs=in_specs,
-            out_specs=anym,
+            out_specs=vmem,
             scratch_shapes=edges + [
                 pltpu.VMEM((ROWS, LB, COLS), f32),
                 pltpu.VMEM((ROUNDS, NB, COLS), f32),
                 pltpu.VMEM((ROUNDS, NB, COLS), f32),
                 pltpu.VMEM((ROWS * LB, COLS), f32),
-                pltpu.VMEM((LB, ROWS, COLS), f32),
             ] + weights + [
                 dma((10,)), dma((4,)), dma((4,)), dma((2, ROUNDS)),
                 dma((ROUNDS, PEERS)), dma((ROUNDS, PEERS)), dma((ROUNDS, PEERS)), dma((ROUNDS, PEERS)),
-                dma((ROUNDS,)),
             ],
-            compiler_params=pltpu.CompilerParams(collective_id=1, has_side_effects=True, vmem_limit_bytes=62 * 2**20),
+            compiler_params=pltpu.CompilerParams(collective_id=1, has_side_effects=True, vmem_limit_bytes=58 * 2**20),
         )(*args[1:]))
 
     packed, flag = pl.pallas_call(
         sea_kernel,
-        out_shape=(shape, pltpu.VMEM((8, COLS), f32)),
+        out_shape=(pltpu.VMEM((LB, ROWS, COLS), f32), pltpu.VMEM((8, COLS), f32)),
         in_specs=in_specs,
-        out_specs=(anym, vmem),
+        out_specs=(vmem, vmem),
         scratch_shapes=edges + [
             pltpu.VMEM((TILES, LB, COLS), f32),
             pltpu.VMEM((EXT, LB, COLS), f32),
@@ -626,17 +609,16 @@
             pltpu.VMEM((7, NB, COLS), f32),
             pltpu.VMEM((ROWS * LB, COLS), f32),
             pltpu.VMEM((2 * LB, EXT * COLS), f32),
-            pltpu.VMEM((LB, ROWS, COLS), f32),
         ] + weights + [
             pltpu.VMEM((4, 8, COLS), f32),
             pltpu.VMEM((4, 8, COLS), f32),
             dma((10,)), dma((4,)), dma((4,)),
             dma((TILES,)), dma((7, PEERS)), dma((7, PEERS)), dma((TILES,)),
-            dma((8,)), dma((2, 4)), dma((2, 4)),
+            dma((2, 4)), dma((2, 4)),
         ],
-        compiler_params=pltpu.CompilerParams(collective_id=0, has_side_effects=True, vmem_limit_bytes=62 * 2**20),
+        compiler_params=pltpu.CompilerParams(collective_id=0, has_side_effects=True, vmem_limit_bytes=58 * 2**20),
     )(*operands)
-    return lax.cond(flag[0, 0] > 0.0, whole, lambda args: finish(args[0]), (packed,) + operands)
+    return lax.cond(flag[0, 0] > 0.0, whole, lambda args: args[0], (packed,) + operands)
 
 
 def solution(mesh):

time: 109 us -> 104 us (0.954)
  Pallas kernels: 107 us -> 101 us
  local copies, waits for them, and re-layouts: 0.53 us -> 2.72 us
    pallas_call x2 -> x1, Pallas kernels: 107 us -> 101 us  [local(): pl.pallas_call(sea_kernel, out_shape=(pltpu.VMEM((LB, ROWS, COLS), f32),...]
    unnamed x10 -> x11, local copies, waits for them, and re-layouts: 0.02 us -> 2.21 us
where the time goes in v3:
time: 104 us
  Pallas kernels  101 us (97%)
  local copies, waits for them, and re-layouts  2.72 us (3%)
    pallas_call x1, Pallas kernels, local(): pl.pallas_call(sea_kernel, out_shape=(pltpu.VMEM((LB, ROWS, COLS), f32),...  101 us
    unnamed x11, local copies, waits for them, and re-layouts  2.21 us

profile of v3, /device:TPU:1, one launch (start us, length us, event | category | flops | bytes accessed | tf_op | source)
XLA Modules:
  0.0 104.2 jit_solution(5728470696856382670)
XLA Ops:
  0.0 0.0 copy-start
  0.0 0.0 copy-start.1
  0.0 0.0 copy-start.2
  0.0 0.0 copy-start.3
  0.0 0.0 copy-start.4
  0.0 100.8 %shard_map.84 = (f32[144,64,128]{2,1,0:T(8,128)S(1)}, f32[8,128]{1,0:T(8,128)S(1)}) custom-call(f32[144,64,128]{2,1,0:T(8,128)} %x.1, s32[64,128]{1,0:T(8,128)} %mask.1, f32[144,128]{1,0:T(8,128)} %constant.7.clone.cosv, f32[144,128]{1,0:T(8,128)} %constant.8.clone.sinv, f32[9,128]{1,0:T(8,128)} %bitcast.3, f32[9,128]{1,0:T(8,128)} %bitcast.5, ...), custom_call_target="tpu_custom_call" | custom-call | tf_op jit(solution)/shard_map/pallas_call | solution.py:597
  100.8 0.5 slice.3
  102.0 0.0 copy-done
  102.0 0.0 copy-done.1
  102.0 0.0 copy-done.2
  102.0 0.0 copy-done.3
  102.0 0.0 copy-done.4
  102.0 2.2 %copy.14 = f32[144,64,128]{2,1,0:T(8,128)} copy(f32[144,64,128]{2,1,0:T(8,128)S(1)} %get-tuple-element.37) | data formatting | bytes 9437184
  (1 shorter events, 0.0 us)
Async XLA Ops:
  0.0 102.0 %copy-start = (f32[144,128]{1,0:T(8,128)S(1)}, f32[144,128]{1,0:T(8,128)}, u32[]{:S(2)}) copy-start(f32[144,128]{1,0:T(8,128)} %constant.8.clone.sinv) | copy-start | bytes 221188
  0.0 102.0 %copy-start.1 = (f32[144,128]{1,0:T(8,128)S(1)}, f32[144,128]{1,0:T(8,128)}, u32[]{:S(2)}) copy-start(f32[144,128]{1,0:T(8,128)} %constant.7.clone.cosv) | copy-start | bytes 221188
  0.0 102.0 %copy-start.2 = (s32[64,128]{1,0:T(8,128)S(1)}, s32[64,128]{1,0:T(8,128)}, u32[]{:S(2)}) copy-start(s32[64,128]{1,0:T(8,128)} %mask.1) | copy-start | bytes 98308
  0.0 102.0 %copy-start.3 = (f32[1152]{0:T(1024)S(1)}, f32[1152]{0:T(1024)}, u32[]{:S(2)}) copy-start(f32[1152]{0:T(1024)} %param.12) | copy-start | bytes 13828
  0.0 102.0 %copy-start.4 = (f32[1152]{0:T(1024)S(1)}, f32[1152]{0:T(1024)}, u32[]{:S(2)}) copy-start(f32[1152]{0:T(1024)} %param.13) | copy-start | bytes 13828

commit v4 on v3

--- a/solution.py
+++ b/solution.py
@@ -232,10 +232,11 @@
 SPLIT = 80
 
 
-def sea_kernel(x, mask, cosv, sinv, grow, band, kg, kl, out, flag,
+def sea_kernel(x, mask_at, cos_at, sin_at, grow_at, band_at, kg, kl, out, flag,
                fin, seab, mlo, mhi, sent, extra, halves, place, hole_at, got, fresh, back, total,
                kgv, klv, growb, bandb, state, square, flx, flz,
-               load_sem, halo_send, halo_recv, fs, fr, bs, br, fls, flr):
+               load_sem, halo_send, halo_recv, fs, fr, bs, br, fls, flr, first_sem,
+               mask, cosv, sinv, grow, band, small_sem):
     me = lax.axis_index("bins")
     space = lax.axis_index("space")
     up = lax.rem(space + 1, SLABS)
@@ -258,26 +259,39 @@
     for other in [up, down] + [x_peer(i) for i in (1, 2, 3)] + [z_peer(i) for i in (1, 2, 3)]:
         pl.semaphore_signal(barrier, inc=1, device_id=(me, other), device_id_type=MESH)
 
+    small = [pltpu.make_async_copy(source, target, small_sem.at[i]) for i, (source, target) in enumerate(
+        ((mask_at, mask), (cos_at, cosv), (sin_at, sinv), (grow_at, grow), (band_at, band)))]
+    for copy in small:
+        copy.start()
+
     def load(q):
         return pltpu.make_async_copy(x.at[:, pl.ds(8 * q, 8), :], fin.at[:, pl.ds(8 * q + 8, 8), :], load_sem.at[q])
 
-    for q in (1, 2, 3, 4, 5, 6, 0, 7):
+    def load_part(q, lo, hi):
+        return pltpu.make_async_copy(x.at[pl.ds(lo, hi - lo), pl.ds(8 * q, 8), :], fin.at[pl.ds(lo, hi - lo), pl.ds(8 * q + 8, 8), :],
+                                     load_sem.at[q] if lo else first_sem.at[q])
+
+    for lo, hi in ((0, SPLIT), (SPLIT, LB)):
+        for q in (1, 2, 3, 4):
+            load_part(q, lo, hi).start()
+    for q in (5, 6, 0, 7):
         load(q).start()
     weights = [pltpu.make_async_copy(kg, kgv, load_sem.at[8]), pltpu.make_async_copy(kl, klv, load_sem.at[9])]
 
+    small[0].wait()
     for q in range(ROWS // 8):
         sea = mask[8 * q:8 * q + 8, :].astype(f32)
         for i in range(8):
             seab[8 + 8 * q + i] = jnp.broadcast_to(sea[i:i + 1, :], (8, COLS))
 
     halos = [
-        pltpu.make_async_remote_copy(x.at[:, pl.ds(56, 8), :], fin.at[:, pl.ds(0, 8), :], halo_send.at[0], halo_recv.at[0],
+        pltpu.make_async_remote_copy(x.at[:, pl.ds(60, 4), :], fin.at[:, pl.ds(4, 4), :], halo_send.at[0], halo_recv.at[0],
                                      device_id=(me, up), device_id_type=MESH),
-        pltpu.make_async_remote_copy(x.at[:, pl.ds(0, 8), :], fin.at[:, pl.ds(72, 8), :], halo_send.at[1], halo_recv.at[1],
+        pltpu.make_async_remote_copy(x.at[:, pl.ds(0, 4), :], fin.at[:, pl.ds(72, 4), :], halo_send.at[1], halo_recv.at[1],
                                      device_id=(me, down), device_id_type=MESH),
-        pltpu.make_async_remote_copy(mask.at[pl.ds(56, 8), :], mlo, halo_send.at[2], halo_recv.at[2],
+        pltpu.make_async_remote_copy(mask_at.at[pl.ds(56, 8), :], mlo, halo_send.at[2], halo_recv.at[2],
                                      device_id=(me, up), device_id_type=MESH),
-        pltpu.make_async_remote_copy(mask.at[pl.ds(0, 8), :], mhi, halo_send.at[3], halo_recv.at[3],
+        pltpu.make_async_remote_copy(mask_at.at[pl.ds(0, 8), :], mhi, halo_send.at[3], halo_recv.at[3],
                                      device_id=(me, down), device_id_type=MESH),
     ]
     inside_lo = (space > 0).astype(f32)
@@ -382,11 +396,13 @@
 
     ready = set()
     over = assign(0)
+    for copy in small[1:]:
+        copy.wait()
     for p, g in enumerate(ORDER):
         for q in range(max(2 * g - 1, 0), min(2 * g + 3, 8)):
-            if q not in ready:
+            if q not in ready and p > 0:
                 load(q).wait()
-                ready.add(q)
+            ready.add(q)
         if p == 2:
             for h in halos:
                 h.wait_recv()
@@ -395,6 +411,9 @@
                 for i in range(8):
                     seab[q + i] = jnp.broadcast_to(sea[i:i + 1, :], (8, COLS))
         for lo, hi in ((0, SPLIT), (SPLIT, LB)) if p == 0 else ((0, LB),):
+            if p == 0:
+                for q in (1, 2, 3, 4):
+                    load_part(q, lo, hi).wait()
             propagate(p, lo, hi)
             if p == 0 and lo == 0:
                 pl.semaphore_wait(barrier, PEERS + 7)
@@ -597,7 +616,7 @@
     packed, flag = pl.pallas_call(
         sea_kernel,
         out_shape=(pltpu.VMEM((LB, ROWS, COLS), f32), pltpu.VMEM((8, COLS), f32)),
-        in_specs=in_specs,
+        in_specs=[anym] * 8,
         out_specs=(vmem, vmem),
         scratch_shapes=edges + [
             pltpu.VMEM((TILES, LB, COLS), f32),
@@ -614,7 +633,13 @@
             pltpu.VMEM((4, 8, COLS), f32),
             dma((10,)), dma((4,)), dma((4,)),
             dma((TILES,)), dma((7, PEERS)), dma((7, PEERS)), dma((TILES,)),
-            dma((2, 4)), dma((2, 4)),
+            dma((2, 4)), dma((2, 4)), dma((8,)),
+            pltpu.VMEM((ROWS, COLS), i32),
+            pltpu.VMEM((LB, COLS), f32),
+            pltpu.VMEM((LB, COLS), f32),
+            pltpu.VMEM((NB // COLS, COLS), f32),
+            pltpu.VMEM((NB // COLS, COLS), f32),
+            dma((5,)),
         ],
         compiler_params=pltpu.CompilerParams(collective_id=0, has_side_effects=True, vmem_limit_bytes=58 * 2**20),
     )(*operands)

time: 104 us -> 103 us (level)
  Pallas kernels: 101 us -> 99.6 us
    pallas_call x1, Pallas kernels: 101 us -> 99.6 us  [local(): pl.pallas_call(sea_kernel, out_shape=(pltpu.VMEM((LB, ROWS, COLS), f32),...]
where the time goes in v4:
time: 103 us
  Pallas kernels  99.6 us (97%)
  local copies, waits for them, and re-layouts  2.72 us (3%)
    pallas_call x1, Pallas kernels, local(): pl.pallas_call(sea_kernel, out_shape=(pltpu.VMEM((LB, ROWS, COLS), f32),...  99.6 us
    unnamed x11, local copies, waits for them, and re-layouts  2.21 us

profile of v4, /device:TPU:1, one launch (start us, length us, event | category | flops | bytes accessed | tf_op | source)
XLA Modules:
  0.0 103.1 jit_solution(9961645125435432773)
XLA Ops:
  0.0 0.0 copy-start
  0.0 0.0 copy-start.1
  0.0 0.0 copy-start.2
  0.0 0.0 copy-start.3
  0.0 0.0 copy-start.4
  0.0 99.6 %shard_map.84 = (f32[144,64,128]{2,1,0:T(8,128)S(1)}, f32[8,128]{1,0:T(8,128)S(1)}) custom-call(f32[144,64,128]{2,1,0:T(8,128)} %x.1, s32[64,128]{1,0:T(8,128)} %mask_at.1, f32[144,128]{1,0:T(8,128)} %constant.7.clone.cos_at, f32[144,128]{1,0:T(8,128)} %constant.8.clone.sin_at, f32[9,128]{1,0:T(8,128)} %bitcast.3, f32[9,128]{1,0:T(8,128)} %bitcast.5, ...), custom_call_target="tpu_custom_call" | custom-call | tf_op jit(solution)/shard_map/pallas_call | solution.py:616
  99.7 0.5 slice.3
  100.9 0.0 copy-done
  100.9 0.0 copy-done.1
  100.9 0.0 copy-done.2
  100.9 0.0 copy-done.3
  100.9 0.0 copy-done.4
  100.9 2.2 %copy.14 = f32[144,64,128]{2,1,0:T(8,128)} copy(f32[144,64,128]{2,1,0:T(8,128)S(1)} %get-tuple-element.37) | data formatting | bytes 9437184
  (1 shorter events, 0.0 us)
Async XLA Ops:
  0.0 100.9 %copy-start = (f32[144,128]{1,0:T(8,128)S(1)}, f32[144,128]{1,0:T(8,128)}, u32[]{:S(2)}) copy-start(f32[144,128]{1,0:T(8,128)} %constant.8.clone.sin_at) | copy-start | bytes 221188
  0.0 100.9 %copy-start.1 = (f32[144,128]{1,0:T(8,128)S(1)}, f32[144,128]{1,0:T(8,128)}, u32[]{:S(2)}) copy-start(f32[144,128]{1,0:T(8,128)} %constant.7.clone.cos_at) | copy-start | bytes 221188
  0.0 100.9 %copy-start.2 = (s32[64,128]{1,0:T(8,128)S(1)}, s32[64,128]{1,0:T(8,128)}, u32[]{:S(2)}) copy-start(s32[64,128]{1,0:T(8,128)} %mask_at.1) | copy-start | bytes 98308
  0.0 100.9 %copy-start.3 = (f32[1152]{0:T(1024)S(1)}, f32[1152]{0:T(1024)}, u32[]{:S(2)}) copy-start(f32[1152]{0:T(1024)} %param.12) | copy-start | bytes 13828
  0.0 100.9 %copy-start.4 = (f32[1152]{0:T(1024)S(1)}, f32[1152]{0:T(1024)}, u32[]{:S(2)}) copy-start(f32[1152]{0:T(1024)} %param.13) | copy-start | bytes 13828

commit v5 on v4

--- a/solution.py
+++ b/solution.py
@@ -229,7 +229,7 @@
 BASE = 13
 EXT = 3
 TILES = BASE * 4
-SPLIT = 80
+SPLIT = 96
 
 
 def sea_kernel(x, mask_at, cos_at, sin_at, grow_at, band_at, kg, kl, out, flag,
@@ -343,7 +343,7 @@
             sent[pl.ds(BASE * p, BASE), pl.ds(b0, 8), :] = field[:BASE]
             extra[:, pl.ds(b0, 8), :] = field[BASE:]
             return carry
-        lax.fori_loop(0, (hi - lo) // 8, tile, 0, unroll=2)
+        lax.fori_loop(0, (hi - lo) // 8, tile, 0, unroll=3)
         for k in range(EXT):
             cells = extra[k, lo:hi, :]
             high = cells.astype(bf16)

time: 103 us -> 103 us (level)
  no operation moved by 1% of the time
where the time goes in v5:
time: 103 us
  Pallas kernels  98.9 us (96%)
  local copies, waits for them, and re-layouts  2.72 us (3%)
    pallas_call x1, Pallas kernels, local(): pl.pallas_call(sea_kernel, out_shape=(pltpu.VMEM((LB, ROWS, COLS), f32),...  98.9 us
    unnamed x11, local copies, waits for them, and re-layouts  2.21 us

profile of v5, /device:TPU:1, one launch (start us, length us, event | category | flops | bytes accessed | tf_op | source)
XLA Modules:
  0.0 102.5 jit_solution(10448341744037527040)
XLA Ops:
  0.0 0.0 copy-start
  0.0 0.0 copy-start.1
  0.0 0.0 copy-start.2
  0.0 0.0 copy-start.3
  0.0 0.0 copy-start.4
  0.0 98.9 %shard_map.84 = (f32[144,64,128]{2,1,0:T(8,128)S(1)}, f32[8,128]{1,0:T(8,128)S(1)}) custom-call(f32[144,64,128]{2,1,0:T(8,128)} %x.1, s32[64,128]{1,0:T(8,128)} %mask_at.1, f32[144,128]{1,0:T(8,128)} %constant.7.clone.cos_at, f32[144,128]{1,0:T(8,128)} %constant.8.clone.sin_at, f32[9,128]{1,0:T(8,128)} %bitcast.3, f32[9,128]{1,0:T(8,128)} %bitcast.5, ...), custom_call_target="tpu_custom_call" | custom-call | tf_op jit(solution)/shard_map/pallas_call | solution.py:616
  98.9 0.5 slice.3
  100.1 0.0 copy-done
  100.1 0.0 copy-done.1
  100.1 0.0 copy-done.2
  100.1 0.0 copy-done.3
  100.2 0.0 copy-done.4
  100.2 0.2 conditional.1
  100.4 2.2 %copy.14 = f32[144,64,128]{2,1,0:T(8,128)} copy(f32[144,64,128]{2,1,0:T(8,128)S(1)} %get-tuple-element.37) | data formatting | bytes 9437184
Async XLA Ops:
  0.0 100.1 %copy-start = (f32[144,128]{1,0:T(8,128)S(1)}, f32[144,128]{1,0:T(8,128)}, u32[]{:S(2)}) copy-start(f32[144,128]{1,0:T(8,128)} %constant.8.clone.sin_at) | copy-start | bytes 221188
  0.0 100.1 %copy-start.1 = (f32[144,128]{1,0:T(8,128)S(1)}, f32[144,128]{1,0:T(8,128)}, u32[]{:S(2)}) copy-start(f32[144,128]{1,0:T(8,128)} %constant.7.clone.cos_at) | copy-start | bytes 221188
  0.0 100.1 %copy-start.2 = (s32[64,128]{1,0:T(8,128)S(1)}, s32[64,128]{1,0:T(8,128)}, u32[]{:S(2)}) copy-start(s32[64,128]{1,0:T(8,128)} %mask_at.1) | copy-start | bytes 98308
  0.0 100.1 %copy-start.3 = (f32[1152]{0:T(1024)S(1)}, f32[1152]{0:T(1024)}, u32[]{:S(2)}) copy-start(f32[1152]{0:T(1024)} %param.12) | copy-start | bytes 13828
  0.0 100.1 %copy-start.4 = (f32[1152]{0:T(1024)S(1)}, f32[1152]{0:T(1024)}, u32[]{:S(2)}) copy-start(f32[1152]{0:T(1024)} %param.13) | copy-start | bytes 13828
